TPU v7x, 32 devices: a whole 2x2x4 slice. The times are simulated.
32 devices in a mesh: dp: 16 (over z, y, core), factor: 2 (over x).
Axes of the slice: x: 2, y: 2, z: 4, core: 2. Of those that a mesh axis runs over, the one named last changes fastest.
Arguments:
- grad_out: bfloat16 [16, 128, 14336], P('dp', None, 'factor'), may hold values from -6 to 6
- act_in: bfloat16 [16, 128, 4096], P('dp', None, 'factor'), may hold values from -6 to 6
- basis_out: bfloat16 [14336, 14336], P('factor', 'dp'), may hold values from -0.046875 to 0.046875
- basis_in: bfloat16 [4096, 4096], P('factor', 'dp'), may hold values from -0.09375 to 0.09375
- eigen_vals: bfloat16 [14336, 4096], P('dp'), may hold values from 0.25 to 4
- query_out: bfloat16 [16, 8, 14336], P(None, None, 'factor'), may hold values from -0.01171875 to 0.01171875
- query_in: bfloat16 [16, 8, 4096], P(None, None, 'factor'), may hold values from -0.01171875 to 0.01171875
Outputs:
- scores: float32 [16, 16], P('factor')
All inputs are finite; a program needn't handle non-finite values.
Results may differ from a plain program's by a relative error of at most 0.023.
Values may be sent and summed in bfloat16 or wider, within the bound.
A program may use at most 128 MiB of HBM per device.

v0:
```python
import jax
import jax.numpy as jnp
from jax import lax
from jax.sharding import PartitionSpec as P


def shards(grad_out, act_in, basis_out, basis_in, eigen_vals, query_out, query_in):
    shard_part = lax.all_gather(grad_out, "dp", axis=0, tiled=True)
    flattened = shard_part.reshape(-1, shard_part.shape[2])
    product = jnp.dot(flattened, basis_out, preferred_element_type=jnp.float32)
    partial_value = product.reshape(shard_part.shape[0], shard_part.shape[1], -1)
    grad_sum = lax.psum_scatter(
        partial_value.astype(jnp.bfloat16), "factor", scatter_dimension=0, tiled=True
    )
    shard_part = lax.all_gather(act_in, "dp", axis=0, tiled=True)
    flattened = shard_part.reshape(-1, shard_part.shape[2])
    product = jnp.dot(flattened, basis_in, preferred_element_type=jnp.float32)
    act_part = product.reshape(shard_part.shape[0], shard_part.shape[1], -1)
    act_sum = lax.psum_scatter(
        act_part.astype(jnp.bfloat16), "factor", scatter_dimension=0, tiled=True
    )
    act_rot = lax.all_gather(act_sum, "dp", axis=2, tiled=True)
    query_part = jnp.einsum("qrk,ki->qri", query_out, basis_out, preferred_element_type=jnp.float32)
    value_part = jnp.einsum("qrk,kj->qrj", query_in, basis_in, preferred_element_type=jnp.float32)
    query_rot, value_sum = (
        lax.psum(query_part.astype(jnp.bfloat16), "factor").astype(jnp.float32),
        lax.psum(value_part.astype(jnp.bfloat16), "factor").astype(jnp.float32),
    )
    value_rot = lax.all_gather(value_sum.astype(jnp.bfloat16), "dp", axis=2, tiled=True)
    query_count = value_rot.shape[0]
    rank_count = value_rot.shape[1]
    value_mat = value_rot.reshape(query_count * rank_count, value_rot.shape[2])
    eigen_float = eigen_vals.astype(jnp.float32)

    def per_sequence(operands):
        contracted = lax.dot_general(
            operands[0], operands[1], (((0,), (0,)), ((), ())), preferred_element_type=jnp.float32
        )
        scaled = (contracted / eigen_float).astype(jnp.bfloat16)
        weighted = lax.dot_general(
            scaled, value_mat, (((1,), (1,)), ((), ())), preferred_element_type=jnp.float32
        )
        weighted = weighted.reshape(weighted.shape[0], query_count, rank_count)
        return jnp.einsum("iqr,qri->q", weighted, query_rot)

    partial_scores = lax.map(per_sequence, (grad_sum, act_rot))
    return lax.psum(partial_scores, "dp")


def solution(mesh):
    in_specs = (
        P("dp", None, "factor"),
        P("dp", None, "factor"),
        P("factor", "dp"),
        P("factor", "dp"),
        P("dp", None),
        P(None, None, "factor"),
        P(None, None, "factor"),
    )
    out_specs = P("factor", None)
    return jax.shard_map(shards, mesh=mesh, in_specs=in_specs, out_specs=out_specs, check_vma=False)
```

profile of v0, /device:TPU:0, one launch (start us, length us, event | category | flops | bytes accessed | tf_op | source)
XLA Modules:
  0.0 484.5 jit_solution(11116595210919433487)
XLA Ops:
  7.4 0.0 copy-start
  7.4 0.0 all-gather.7.cloned.1.call-start
  7.4 0.7 all-gather.7.cloned.1.call-update
  8.1 0.0 all-reduce.3.cloned.1.call-start
  8.1 2.3 convolution_convert_fusion.1
  10.5 0.0 copy-done
  10.5 0.0 copy-start.2
  10.5 7.5 %fusion.23 = bf16[16,8,896]{2,1,0:T(8,128)(2,1)} fusion(bf16[16,8,7168]{2,1,0:T(8,128)(2,1)S(1)} %copy-done, bf16[7168,896]{1,0:T(8,128)(2,1)} %param.11), kind=kOutput, calls=%fused_computation.17 | convolution fusion | flops 1644281856 | bytes 14909440 | tf_op jit(solution)/shard_map/qrk,ki->qri/dot_general | solution.py:23
  17.9 0.0 all-reduce.3.cloned.1.call-update
  18.0 0.0 reduce-scatter.5.cloned.1.call-start
  18.0 70.0 %all-gather.7.cloned.1.call-done = bf16[16,128,2048]{2,1,0:T(8,128)(2,1)} async-done(((bf16[1,128,2048]{2,1,0:T(8,128)(2,1)}), bf16[16,128,2048]{2,1,0:T(8,128)(2,1)}) %all-gather.7.cloned.1.call-update) | async-done | bytes 8388624 | tf_op jit(solution)/shard_map/all_gather | solution.py:15
  88.0 0.0 copy-done.2
  88.0 6.8 %convolution_convert_fusion = bf16[16,128,256]{2,1,0:T(8,128)(2,1)} fusion(bf16[16,128,2048]{2,1,0:T(8,128)(2,1)} %all-gather.7.cloned.1.call-done, bf16[2048,256]{1,0:T(8,128)(2,1)S(1)} %copy-done.2), kind=kOutput, calls=%fused_computation.16 | convolution fusion | flops 2148007936 | bytes 10485760 | tf_op jit(solution)/shard_map/dot_general | solution.py:17
  94.8 0.0 reduce-scatter.5.cloned.1.call-update
  94.8 0.0 all-gather.5.cloned.1.call-start
  94.9 0.7 all-gather.5.cloned.1.call-update
  95.6 0.0 all-gather.11.cloned.1.call-start
  95.6 0.0 all-reduce.3.cloned.1.call-done
  95.6 0.6 all-gather.11.cloned.1.call-update
  96.3 0.0 all-gather.9.cloned.1.call-start
  96.3 17.0 %reduce-scatter.5.cloned.1.call-done = bf16[8,128,256]{2,1,0:T(8,128)(2,1)} async-done(((bf16[16,128,256]{2,1,0:T(8,128)(2,1)}), bf16[8,128,256]{2,1,0:T(8,128)(2,1)}) %reduce-scatter.5.cloned.1.call-update) | async-done | bytes 524304 | tf_op jit(solution)/shard_map/reduce_scatter | solution.py:19
  113.4 0.0 all-gather.9.cloned.1.call-update
  113.4 0.2 reduce-scatter.3.cloned.1.call-start
  113.6 130.3 %all-gather.5.cloned.1.call-done = bf16[16,128,7168]{2,1,0:T(8,128)(2,1)} async-done(((bf16[1,128,7168]{2,1,0:T(8,128)(2,1)}), bf16[16,128,7168]{2,1,0:T(8,128)(2,1)}) %all-gather.5.cloned.1.call-update) | async-done | bytes 29360144 | tf_op jit(solution)/shard_map/all_gather | solution.py:8
  244.0 38.7 %fusion.20 = bf16[16,128,896]{2,1,0:T(8,128)(2,1)} fusion(bf16[16,128,7168]{2,1,0:T(8,128)(2,1)} %all-gather.5.cloned.1.call-done, bf16[7168,896]{1,0:T(8,128)(2,1)} %param.11), kind=kOutput, calls=%fused_computation.15 | convolution fusion | flops 26308509696 | bytes 45875200 | tf_op jit(solution)/shard_map/dot_general | solution.py:10
  282.6 0.0 reduce-scatter.3.cloned.1.call-update
  282.7 0.0 copy-start.3
  282.7 11.7 %convert_element_type.25 = f32[896,4096]{1,0:T(8,128)} convert(bf16[896,4096]{1,0:T(8,128)(2,1)} %param.13) | non-fusion elementwise | flops 3670016 | bytes 22020096 | tf_op jit(solution)/shard_map/convert_element_type | solution.py:33
  294.3 0.0 copy-done.3
  294.4 0.0 all-gather.11.cloned.1.call-done
  294.4 68.2 %all-gather.9.cloned.1.call-done = bf16[8,128,4096]{2,1,0:T(8,128)(2,1)} async-done(((bf16[8,128,256]{2,1,0:T(8,128)(2,1)}), bf16[8,128,4096]{2,1,0:T(8,128)(2,1)}) %all-gather.9.cloned.1.call-update) | async-done | bytes 8388624 | tf_op jit(solution)/shard_map/all_gather | solution.py:22
  362.6 0.0 reduce-scatter.3.cloned.1.call-done
  362.6 82.6 %while.10 = (s32[]{:T(128)}, f32[8,16]{1,0:T(8,128)S(1)}, bf16[8,128,896]{2,1,0:T(8,128)(2,1)}, bf16[8,128,4096]{2,1,0:T(8,128)(2,1)}, f32[896,4096]{1,0:T(8,128...) while((s32[]{:T(128)}, f32[8,16]{1,0:T(8,128)S(1)}, ...), condition=%wide.region_5.6_spmd, body=%wide.region_4.5_spmd.sunk | while | flops 1886617600 | bytes 17466664 | solution.py:46
  362.6 10.3 %fusion.40 = f32[16]{0:T(128)S(1)} fusion(bf16[128,4096]{1,0:T(8,128)(2,1)} %get-tuple-element.125, f32[896,4096]{1,0:T(8,128)} %get-tuple-element.124, bf16[8,128,4096]{2,1,0:T(8,128)(2,1)} %get-tuple-element.123, s32[]{:T(128)S(6)} %copy.19, f32[16,8,896]{2,1,0:T(8,128)S(1)} %get-tuple-element.126, bf16[8,128,896]{2,1,0:T(8,128)(2,1)} %get-tuple-element.122), kind=kOutput, calls=%fused_computation.5.clone.1 | convolution fusion | flops 1886617600 | bytes 17466432 | tf_op jit(solution)/shard_map/while/body/eval_jaxpr/dot_general | solution.py:40
  373.0 10.3 %fusion.40 = f32[16]{0:T(128)S(1)} fusion(bf16[128,4096]{1,0:T(8,128)(2,1)} %get-tuple-element.125, f32[896,4096]{1,0:T(8,128)} %get-tuple-element.124, bf16[8,128,4096]{2,1,0:T(8,128)(2,1)} %get-tuple-element.123, s32[]{:T(128)S(6)} %copy.19, f32[16,8,896]{2,1,0:T(8,128)S(1)} %get-tuple-element.126, bf16[8,128,896]{2,1,0:T(8,128)(2,1)} %get-tuple-element.122), kind=kOutput, calls=%fused_computation.5.clone.1 | convolution fusion | flops 1886617600 | bytes 17466432 | tf_op jit(solution)/shard_map/while/body/eval_jaxpr/dot_general | solution.py:40
  383.3 10.3 %fusion.40 = f32[16]{0:T(128)S(1)} fusion(bf16[128,4096]{1,0:T(8,128)(2,1)} %get-tuple-element.125, f32[896,4096]{1,0:T(8,128)} %get-tuple-element.124, bf16[8,128,4096]{2,1,0:T(8,128)(2,1)} %get-tuple-element.123, s32[]{:T(128)S(6)} %copy.19, f32[16,8,896]{2,1,0:T(8,128)S(1)} %get-tuple-element.126, bf16[8,128,896]{2,1,0:T(8,128)(2,1)} %get-tuple-element.122), kind=kOutput, calls=%fused_computation.5.clone.1 | convolution fusion | flops 1886617600 | bytes 17466432 | tf_op jit(solution)/shard_map/while/body/eval_jaxpr/dot_general | solution.py:40
  393.6 10.3 %fusion.40 = f32[16]{0:T(128)S(1)} fusion(bf16[128,4096]{1,0:T(8,128)(2,1)} %get-tuple-element.125, f32[896,4096]{1,0:T(8,128)} %get-tuple-element.124, bf16[8,128,4096]{2,1,0:T(8,128)(2,1)} %get-tuple-element.123, s32[]{:T(128)S(6)} %copy.19, f32[16,8,896]{2,1,0:T(8,128)S(1)} %get-tuple-element.126, bf16[8,128,896]{2,1,0:T(8,128)(2,1)} %get-tuple-element.122), kind=kOutput, calls=%fused_computation.5.clone.1 | convolution fusion | flops 1886617600 | bytes 17466432 | tf_op jit(solution)/shard_map/while/body/eval_jaxpr/dot_general | solution.py:40
  404.0 10.3 %fusion.40 = f32[16]{0:T(128)S(1)} fusion(bf16[128,4096]{1,0:T(8,128)(2,1)} %get-tuple-element.125, f32[896,4096]{1,0:T(8,128)} %get-tuple-element.124, bf16[8,128,4096]{2,1,0:T(8,128)(2,1)} %get-tuple-element.123, s32[]{:T(128)S(6)} %copy.19, f32[16,8,896]{2,1,0:T(8,128)S(1)} %get-tuple-element.126, bf16[8,128,896]{2,1,0:T(8,128)(2,1)} %get-tuple-element.122), kind=kOutput, calls=%fused_computation.5.clone.1 | convolution fusion | flops 1886617600 | bytes 17466432 | tf_op jit(solution)/shard_map/while/body/eval_jaxpr/dot_general | solution.py:40
  414.3 10.3 %fusion.40 = f32[16]{0:T(128)S(1)} fusion(bf16[128,4096]{1,0:T(8,128)(2,1)} %get-tuple-element.125, f32[896,4096]{1,0:T(8,128)} %get-tuple-element.124, bf16[8,128,4096]{2,1,0:T(8,128)(2,1)} %get-tuple-element.123, s32[]{:T(128)S(6)} %copy.19, f32[16,8,896]{2,1,0:T(8,128)S(1)} %get-tuple-element.126, bf16[8,128,896]{2,1,0:T(8,128)(2,1)} %get-tuple-element.122), kind=kOutput, calls=%fused_computation.5.clone.1 | convolution fusion | flops 1886617600 | bytes 17466432 | tf_op jit(solution)/shard_map/while/body/eval_jaxpr/dot_general | solution.py:40
  424.6 10.3 %fusion.40 = f32[16]{0:T(128)S(1)} fusion(bf16[128,4096]{1,0:T(8,128)(2,1)} %get-tuple-element.125, f32[896,4096]{1,0:T(8,128)} %get-tuple-element.124, bf16[8,128,4096]{2,1,0:T(8,128)(2,1)} %get-tuple-element.123, s32[]{:T(128)S(6)} %copy.19, f32[16,8,896]{2,1,0:T(8,128)S(1)} %get-tuple-element.126, bf16[8,128,896]{2,1,0:T(8,128)(2,1)} %get-tuple-element.122), kind=kOutput, calls=%fused_computation.5.clone.1 | convolution fusion | flops 1886617600 | bytes 17466432 | tf_op jit(solution)/shard_map/while/body/eval_jaxpr/dot_general | solution.py:40
  435.0 10.3 %fusion.40 = f32[16]{0:T(128)S(1)} fusion(bf16[128,4096]{1,0:T(8,128)(2,1)} %get-tuple-element.125, f32[896,4096]{1,0:T(8,128)} %get-tuple-element.124, bf16[8,128,4096]{2,1,0:T(8,128)(2,1)} %get-tuple-element.123, s32[]{:T(128)S(6)} %copy.19, f32[16,8,896]{2,1,0:T(8,128)S(1)} %get-tuple-element.126, bf16[8,128,896]{2,1,0:T(8,128)(2,1)} %get-tuple-element.122), kind=kOutput, calls=%fused_computation.5.clone.1 | convolution fusion | flops 1886617600 | bytes 17466432 | tf_op jit(solution)/shard_map/while/body/eval_jaxpr/dot_general | solution.py:40
  445.3 0.0 copy-start.1
  445.3 31.8 %psum.23 = f32[8,16]{1,0:T(8,128)} all-reduce(f32[8,16]{1,0:T(8,128)S(1)} %get-tuple-element.42), channel_id=1, replica_groups=mesh['dp'=16,'factor'=2] {'dp'}, use_global_device_ids=true, to_apply=%region_6.7 | all-reduce | flops 128 | bytes 1024 | tf_op jit(solution)/shard_map/psum | solution.py:47
  477.1 0.0 copy-done.1
  (10 shorter events, 0.2 us)
Async XLA Ops:
  7.4 3.1 copy-start
  7.4 80.6 %all-gather.7.cloned.1.call-start = ((), (), s32[]{:S(2)}) async-start(), calls=%async_computation.4 | async-start | bytes 8912896 | tf_op jit(solution)/shard_map/all_gather | solution.py:15
  8.1 87.5 %all-reduce.3.cloned.1.call-start = ((), (), s32[]{:S(2)}) async-start(), calls=%async_computation.8 | async-start | bytes 589824 | tf_op jit(solution)/shard_map/psum | solution.py:27
  10.5 77.5 %copy-start.2 = (bf16[2048,256]{1,0:T(8,128)(2,1)S(1)}, bf16[2048,256]{1,0:T(8,128)(2,1)}, u32[]{:S(2)}) copy-start(bf16[2048,256]{1,0:T(8,128)(2,1)} %param.12) | copy-start | bytes 3145732
  18.0 95.4 %reduce-scatter.5.cloned.1.call-start = ((), (), s32[]{:S(2)}) async-start(), calls=%async_computation.5 | async-start | bytes 1572864 | tf_op jit(solution)/shard_map/reduce_scatter | solution.py:19
  94.8 149.2 %all-gather.5.cloned.1.call-start = ((), (), s32[]{:S(2)}) async-start(), calls=%async_computation.2 | async-start | bytes 31195136 | tf_op jit(solution)/shard_map/all_gather | solution.py:8
  95.6 198.8 %all-gather.11.cloned.1.call-start = ((), (), s32[]{:S(2)}) async-start(), calls=%async_computation.7 | async-start | bytes 1114112 | tf_op jit(solution)/shard_map/all_gather | solution.py:29
  96.3 266.3 %all-gather.9.cloned.1.call-start = ((), (), s32[]{:S(2)}) async-start(), calls=%async_computation.6 | async-start | bytes 8912896 | tf_op jit(solution)/shard_map/all_gather | solution.py:22
  113.4 249.2 %reduce-scatter.3.cloned.1.call-start = ((), (), s32[]{:S(2)}) async-start(), calls=%async_computation.3 | async-start | bytes 5505024 | tf_op jit(solution)/shard_map/reduce_scatter | solution.py:12
  282.7 11.7 %copy-start.3 = (bf16[16,8,896]{2,1,0:T(8,128)(2,1)S(1)}, bf16[16,8,896]{2,1,0:T(8,128)(2,1)}, u32[]{:S(2)}) copy-start(bf16[16,8,896]{2,1,0:T(8,128)(2,1)} %get-tuple-element.58) | copy-start | bytes 688132
  445.3 31.8 %copy-start.1 = (bf16[16,8,7168]{2,1,0:T(8,128)(2,1)S(1)}, bf16[16,8,7168]{2,1,0:T(8,128)(2,1)}, u32[]{:S(2)}) copy-start(bf16[16,8,7168]{2,1,0:T(8,128)(2,1)} %param.14) | copy-start | bytes 5505028
Sparse Core Ops, SparseCore 0:
  10.4 77.5 all-gather.6
  97.3 146.5 all-gather.4
  246.1 36.7 all-gather.10
  285.0 77.6 all-gather.8
Sparse Core Ops, SparseCore 1:
  18.1 26.3 all-reduce.2
  94.9 18.4 reduce-scatter.4
  282.7 49.0 reduce-scatter.2
where the time goes:
time: 485 us; the launch traced here: 484 us
  waiting for transfers between devices  288 us (59%)
  matrix products  138 us (28%)
  blocking collectives  31.8 us (7%)
  between operations  14.9 us (3%)
  other arithmetic  11.7 us (2%)
    all_gather x1, waiting for transfers between devices, shards(): shard_part = lax.all_gather(grad_out, 'dp', axis=0, tiled=True)  130 us
    dot_general x8, matrix products, per_sequence(): lax.dot_general(scaled, value_mat, (((1,), (1,)), ((), ())), preferred_el...  82.3 us
    all_gather x1, waiting for transfers between devices, shards(): shard_part = lax.all_gather(act_in, 'dp', axis=0, tiled=True)  70 us
    all_gather x1, waiting for transfers between devices, shards(): act_rot = lax.all_gather(act_sum, 'dp', axis=2, tiled=True)  68.2 us
    dot_general x1, matrix products, shards(): product = jnp.dot(flattened, basis_out, preferred_element_type=jnp.float32)  38.7 us
    psum x1, blocking collectives, shards(): return lax.psum(partial_scores, 'dp')  31.8 us
    reduce_scatter x1, waiting for transfers between devices, shards(): lax.psum_scatter(act_part.astype(jnp.bfloat16), 'factor', scatter_dimensi...  17 us
    convert_element_type x1, other arithmetic, shards(): eigen_float = eigen_vals.astype(jnp.float32)  11.7 us
  transfers between devices with their start and end apart: 7, of which 4 were waited for; matrix products, arithmetic and copies ran while one was open for 14% of the time, Pallas kernels for 0%

commit v1 on v0

v1 whole, which is shorter than its diff:
```python
import functools

import jax
import jax.numpy as jnp
from jax import lax
from jax.experimental import pallas as pl
from jax.experimental.pallas import tpu as pltpu
from jax.sharding import PartitionSpec as P

F32 = jnp.float32
BF16 = jnp.bfloat16
MESH = pl.DeviceIdType.MESH
NA = 4
CHUNKS = 2


class Gather:
    def __init__(self, place, nb, own, buf, chunks, sems, wide):
        self.a, self.b, self.c = place
        self.nb, self.own, self.buf, self.chunks, self.wide = nb, own, buf, chunks, wide
        self.recv, self.up, self.down, self.across, self.core = sems
        self.sends = []

    def block(self, a, b, c):
        return (a * self.nb + b) * 2 + c

    def lane(self, m):
        return lax.rem(self.b + m, self.nb)

    def turn(self, n):
        if n == 0:
            return self.a
        if n == 1:
            return self.a + 1 - 2 * lax.rem(self.a, 2)
        if n == 2:
            return lax.rem(self.a + 2, 4)
        return 3 - self.a

    def send(self, src, block, h, sem, dev, conds):
        copy = pltpu.make_async_remote_copy(
            src_ref=src, dst_ref=self.buf(block, h), send_sem=sem, recv_sem=self.recv.at[block, h],
            device_id={"dp": dev}, device_id_type=MESH)
        self.sends.append((copy, conds))
        guard(conds, copy.start)

    def wait(self, block, h):
        other = self.block(self.a, self.b, 1 - self.c)
        pltpu.make_async_remote_copy(
            src_ref=self.buf(block, h), dst_ref=self.buf(block, h), send_sem=self.core.at[0, h],
            recv_sem=self.recv.at[block, h], device_id={"dp": other}, device_id_type=MESH).wait_recv()

    def step_up(self, src, block, h, m, k, conds):
        if k < NA - 1:
            self.send(src, block, h, self.up.at[m, k, h], self.block(self.a + 1, self.b, self.c), conds + [self.a < NA - 1])

    def step_down(self, src, block, h, m, k, conds):
        if k < NA - 1:
            self.send(src, block, h, self.down.at[m, k, h], self.block(self.a - 1, self.b, self.c), conds + [self.a > 0])

    def to_core(self, src, block, h, m, row, conds):
        self.send(src, block, h, self.core.at[m * NA + row, h], self.block(self.a, self.b, 1 - self.c), conds)

    def start(self):
        me = self.block(self.a, self.b, self.c)
        for h in range(self.chunks):
            src = self.own(h)
            self.step_up(src, me, h, 0, 0, [])
            self.step_down(src, me, h, 0, 0, [])
            for m in range(1, self.nb):
                self.send(src, me, h, self.across.at[m - 1, h], self.block(self.a, self.lane(m), self.c), [])
            self.to_core(src, me, h, 0, self.a, [])

    def line(self, k):
        for m in range(self.nb if self.wide else 1):
            for h in range(self.chunks):
                for sign in (-1, 1):
                    row = self.a + sign * (k + 1)
                    cond = row >= 0 if sign < 0 else row < NA
                    block = self.block(row, self.lane(m), self.c)
                    guard([cond], functools.partial(self.wait, block, h))
                    src = self.buf(block, h)
                    if sign < 0:
                        self.step_up(src, block, h, m, k + 1, [cond])
                    else:
                        self.step_down(src, block, h, m, k + 1, [cond])
                    self.to_core(src, block, h, m, row, [cond])

    def rows(self, n):
        block = self.block(self.turn(n), self.b, self.c)
        for h in range(self.chunks):
            for m in range(1, self.nb):
                self.send(self.buf(block, h), block, h, self.across.at[n * (self.nb - 1) + m - 1, h],
                          self.block(self.a, self.lane(m), self.c), [])

    def rows_wait(self, n):
        for m in range(1, self.nb):
            block = self.block(self.turn(n), self.lane(m), self.c)
            for h in range(self.chunks):
                self.wait(block, h)
                src = self.buf(block, h)
                if self.wide:
                    self.step_up(src, block, h, m, 0, [])
                    self.step_down(src, block, h, m, 0, [])
                self.to_core(src, block, h, m, self.turn(n), [])

    def core_wait(self, n, m):
        block = self.block(self.turn(n), self.lane(m), 1 - self.c)
        for h in range(self.chunks):
            self.wait(block, h)

    def finish(self):
        for copy, conds in self.sends:
            guard(conds, copy.wait_send)


def guard(conds, run):
    if not conds:
        run()
        return
    cond = conds[0]
    for more in conds[1:]:
        cond = jnp.logical_and(cond, more)

    @pl.when(cond)
    def _():
        run()


def tiles(width, most):
    start = 0
    while start < width:
        size = min(most, width - start)
        yield start, size
        start += size


def kernel(nb, nf, grad, act, bo, bi, ev, qo, qi, out, gbuf, abuf,
           bo_v, bi_v, slot, re, ev_v, rbuf, pbuf, precv, apart, arecv, gt, qsend, qrecv, vsend, vrecv, qrt, wacc, score, srecv,
           g_recv, g_up, g_down, g_across, g_core, a_recv, a_up, a_down, a_across, a_core,
           r_recv, r_up, r_down, r_across, r_core,
           load_sem, ev_sem, slot_sem, p_send, p_recv, ap_send, ap_recv, q_send, q_recv, v_send, v_recv, s_send, s_recv):
    d = lax.axis_index("dp")
    f = lax.axis_index("factor")
    nd = NA * nb * 2
    c = lax.rem(d, 2)
    b = lax.rem(d // 2, nb)
    a = d // (2 * nb)
    tok, ka = act.shape
    ni = bo.shape[1]
    nj = bi.shape[1]
    nq = qo.shape[0]
    own_n = nd // nf
    rows = tok // CHUNKS

    loads = [(bo, bo_v), (bi, bi_v), (qo, slot.at[0, pl.ds(0, nq)]), (qi, slot.at[1, pl.ds(0, nq), pl.ds(0, ka)])]
    loads = [pltpu.make_async_copy(s, t, load_sem.at[i]) for i, (s, t) in enumerate(loads)]
    for load in loads:
        load.start()

    barrier = pltpu.get_barrier_semaphore()
    peers = [{"dp": (a * nb + b) * 2 + 1 - c}]
    peers += [{"dp": (a * nb + lax.rem(b + m, nb)) * 2 + c} for m in range(1, nb)]
    peers += [{"dp": (lax.rem(a + m, NA) * nb + b) * 2 + c} for m in range(1, NA)]
    peers += [{"factor": lax.rem(f + m, nf)} for m in range(1, nf)]
    for peer in peers:
        pl.semaphore_signal(barrier, inc=1, device_id=peer, device_id_type=MESH)
    pl.semaphore_wait(barrier, len(peers))

    place = (a, b, c)
    A = Gather(place, nb, lambda h: act, lambda k, h: abuf.at[k], 1, (a_recv, a_up, a_down, a_across, a_core), False)
    G = Gather(place, nb, lambda h: grad.at[pl.ds(h * rows, rows)], lambda k, h: gbuf.at[k, pl.ds(h * rows, rows)], CHUNKS,
               (g_recv, g_up, g_down, g_across, g_core), False)
    R = Gather(place, nb, lambda h: rbuf.at[d], lambda k, h: rbuf.at[k], 1, (r_recv, r_up, r_down, r_across, r_core), True)
    A.start()
    G.start()

    def swap(src, dst, send, recv):
        copies = [pltpu.make_async_remote_copy(
            src_ref=src, dst_ref=dst.at[m - 1], send_sem=send.at[m - 1], recv_sem=recv.at[m - 1],
            device_id={"factor": lax.rem(f + m, nf)}, device_id_type=MESH) for m in range(1, nf)]
        for copy in copies:
            copy.start()
        return copies

    for load in loads:
        load.wait()
    for start, size in tiles(ni, 256):
        qsend[:, start:start + size] = jnp.dot(slot[0, :nq, :], bo_v[:, start:start + size], preferred_element_type=F32)
    vsend[...] = jnp.dot(slot[1, :nq, :ka], bi_v[...], preferred_element_type=F32)
    q_copies = swap(qsend, qrecv, q_send, q_recv)
    v_copies = swap(vsend, vrecv, v_send, v_recv)

    def ev_load(k, par):
        return pltpu.make_async_copy(ev.at[:, pl.ds(pl.multiple_of(k * nj, nj), nj)], ev_v.at[par], ev_sem.at[par])

    ev_load(0, 0).start()

    def ev_step(k, carry):
        par = lax.rem(k, 2)

        @pl.when(k + 1 < nd)
        def _():
            ev_load(k + 1, 1 - par).start()

        ev_load(k, par).wait()
        re[k] = 1.0 / ev_v[par].astype(F32)
        return carry

    lax.fori_loop(0, nd, ev_step, 0)

    A.line(0)
    A.rows(1)
    A.rows_wait(0)
    A.line(1)
    A.rows(2)
    A.rows_wait(1)
    A.line(2)
    A.rows(3)
    A.rows_wait(2)
    A.rows_wait(3)

    order = [(n, m) for n in range(NA) for m in range(nb)]

    def pair_of(n, m):
        return G.turn(n) * nb + G.lane(m)

    def slot_load(index, buf, own, width, par):
        n, m = order[index]
        p = pair_of(n, m)
        copies = []
        for e in range(2):
            core = c if e == 0 else 1 - c
            src = own if index == 0 and e == 0 else buf.at[2 * p + core]
            dst = slot.at[par, pl.ds(pl.multiple_of(core * tok, tok), tok)]
            if width is not None:
                dst = slot.at[par, pl.ds(pl.multiple_of(core * tok, tok), tok), pl.ds(0, width)]
            copies.append(pltpu.make_async_copy(src, dst, slot_sem.at[par, e]))
        return copies

    def part_copy(index, half, part, recv, send_sem, recv_sem):
        s = 2 * pair_of(*order[index]) + half
        owner = lax.rem(s, nf)
        q = lax.rem(f - owner + nf, nf) - 1
        q = jnp.maximum(q, 0)
        return owner, s // nf, pltpu.make_async_remote_copy(
            src_ref=part.at[index, pl.ds(half * tok, tok)], dst_ref=recv.at[q, s // nf],
            send_sem=send_sem.at[index, half], recv_sem=recv_sem.at[q, s // nf],
            device_id={"factor": owner}, device_id_type=MESH)

    def part_send(index, part, recv, send_sem, recv_sem):
        for half in range(2):
            owner, _, copy = part_copy(index, half, part, recv, send_sem, recv_sem)
            guard([owner != f], copy.start)

    def part_done(index, part, recv, send_sem, recv_sem):
        for half in range(2):
            owner, _, copy = part_copy(index, half, part, recv, send_sem, recv_sem)
            guard([owner != f], copy.wait_send)

    def part_sum(index, half, j, part, recv, recv_sem):
        total = part[index, half * tok:(half + 1) * tok, :].astype(F32)
        for q in range(nf - 1):
            pltpu.make_async_remote_copy(
                src_ref=recv.at[q, j], dst_ref=recv.at[q, j], send_sem=v_send.at[0], recv_sem=recv_sem.at[q, j],
                device_id={"factor": lax.rem(f + 1, nf)}, device_id_type=MESH).wait_recv()
            total += recv[q, j].astype(F32)
        return total

    for n, m in order:
        A.core_wait(n, m)
    now = slot_load(0, abuf, act, ka, 0)
    for copy in now:
        copy.start()
    for index in range(len(order)):
        par = index % 2
        later = []
        if index + 1 < len(order):
            later = slot_load(index + 1, abuf, act, ka, 1 - par)
            for copy in later:
                copy.start()
        for copy in now:
            copy.wait()
        apart[index] = jnp.dot(slot[par, :, :ka], bi_v[...], preferred_element_type=F32).astype(BF16)
        part_send(index, apart, arecv, ap_send, ap_recv)
        now = later

    for copy in q_copies + v_copies:
        copy.wait()
    qsum = qsend[...]
    vsum = vsend[...]
    for q in range(nf - 1):
        qsum += qrecv[q]
        vsum += vrecv[q]
    qrt[...] = qsum.T
    rbuf[d, own_n * tok:, :] = vsum.astype(BF16)

    G.line(0)
    G.rows(1)

    for index in range(len(order)):
        for half in range(2):
            s = 2 * pair_of(*order[index]) + half

            @pl.when(lax.rem(s, nf) == f)
            def _():
                j = s // nf
                total = part_sum(index, half, j, apart, arecv, ap_recv)
                rbuf[d, pl.ds(pl.multiple_of(j * tok, tok), tok), :] = total.astype(BF16)

    R.start()

    def rotate(par, index):
        def body(k, carry):
            cols = pl.ds(pl.multiple_of(k * 256, 128), 256)
            pbuf[index, :, cols] = jnp.dot(slot[par], bo_v[:, cols], preferred_element_type=F32).astype(BF16)
            return carry

        whole = ni // 256
        lax.fori_loop(0, whole, body, 0)
        if whole * 256 < ni:
            pbuf[index, :, whole * 256:] = jnp.dot(
                slot[par], bo_v[:, whole * 256:], preferred_element_type=F32).astype(BF16)

    def multiply(index):
        n, m = order[index]
        G.core_wait(n, m)
        par = index % 2
        copies = slot_load(index, gbuf, grad, None, par)
        for copy in copies:
            copy.start()
        for copy in copies:
            copy.wait()
        rotate(par, index)
        part_send(index, pbuf, precv, p_send, p_recv)

    def finalize(index):
        for half in range(2):
            s = 2 * pair_of(*order[index]) + half

            @pl.when(lax.rem(s, nf) == f)
            def _():
                j = s // nf
                total = part_sum(index, half, j, pbuf, precv, p_recv)
                gt[j] = total.astype(BF16).astype(F32).T.astype(BF16)

    def score_one(j):
        wacc[...] = jnp.zeros_like(wacc)

        def body(k, carry):
            part = rbuf[k, pl.ds(pl.multiple_of(j * tok, tok), tok), :]
            contracted = jnp.dot(gt[j], part, preferred_element_type=F32)
            scaled = (contracted * re[k]).astype(BF16)
            wacc[...] += lax.dot_general(scaled, rbuf[k, own_n * tok:, :], (((1,), (1,)), ((), ())),
                                         preferred_element_type=F32)
            return carry

        lax.fori_loop(0, nd, body, 0)
        score[0, pl.ds(j, 1), :] = jnp.sum(wacc[...] * qrt[...], axis=0, keepdims=True)

    def score_pairs(first, last):
        def body(index, carry):
            n = index // nb
            m = lax.rem(index, nb)
            row = jnp.where(n == 0, G.turn(0), jnp.where(n == 1, G.turn(1), jnp.where(n == 2, G.turn(2), G.turn(3))))
            p = row * nb + lax.rem(b + m, nb)

            def each(half, carry):
                s = 2 * p + half

                @pl.when(lax.rem(s, nf) == f)
                def _():
                    score_one(s // nf)

                return carry

            return lax.fori_loop(0, 2, each, carry)

        lax.fori_loop(first, last, body, 0)

    multiply(0)
    R.rows_wait(0)
    G.rows_wait(0)
    for m in range(1, nb):
        multiply(m)
    R.line(0)
    G.line(1)
    G.rows(2)
    R.line(1)
    multiply(nb)
    G.rows_wait(1)
    for m in range(1, nb):
        multiply(nb + m)
    R.line(2)
    for index in range(nb):
        finalize(index)
    for n, m in order:
        R.core_wait(n, m)
    G.line(2)
    G.rows(3)
    score_pairs(0, nb)
    multiply(2 * nb)
    G.rows_wait(2)
    for m in range(1, nb):
        multiply(2 * nb + m)
    for index in range(nb, 2 * nb + 1):
        finalize(index)
    score_pairs(nb, 2 * nb + 1)
    multiply(3 * nb)
    for index in range(2 * nb + 1, 3 * nb + 1):
        finalize(index)
    score_pairs(2 * nb + 1, 3 * nb + 1)
    G.rows_wait(3)
    for m in range(1, nb):
        multiply(3 * nb + m)
    for index in range(3 * nb + 1, 4 * nb):
        finalize(index)
    score_pairs(3 * nb + 1, 4 * nb)

    copies = []
    bits = nd.bit_length() - 1
    for k in range(bits):
        step = 1 << k
        peer = d + step * (1 - 2 * lax.rem(d // step, 2))
        copy = pltpu.make_async_remote_copy(
            src_ref=score.at[k], dst_ref=srecv.at[k], send_sem=s_send.at[k], recv_sem=s_recv.at[k],
            device_id={"dp": peer}, device_id_type=MESH)
        copy.start()
        copy.wait_recv()
        score[k + 1] = score[k] + srecv[k]
        copies.append(copy)
    for m in range(1, nf):
        copy = pltpu.make_async_remote_copy(
            src_ref=score.at[bits], dst_ref=srecv.at[bits + m - 1], send_sem=s_send.at[bits + m - 1],
            recv_sem=s_recv.at[bits + m - 1], device_id={"factor": lax.rem(f + m, nf)}, device_id_type=MESH)
        copy.start()
        copies.append(copy)
    out[f] = score[bits]
    for m in range(1, nf):
        copies[bits + m - 1].wait_recv()
        out[lax.rem(f - m + nf, nf)] = srecv[bits + m - 1]
    for copy in copies:
        copy.wait_send()
    A.finish()
    G.finish()
    R.finish()
    for index in range(len(order)):
        part_done(index, apart, arecv, ap_send, ap_recv)
        part_done(index, pbuf, precv, p_send, p_recv)


def shards(nd, nf, grad_out, act_in, basis_out, basis_in, eigen_vals, query_out, query_in):
    nb = nd // (2 * NA)
    tok, kg = grad_out.shape[1:]
    ka = act_in.shape[2]
    ni = basis_out.shape[1]
    nj = basis_in.shape[1]
    queries, rank = query_out.shape[:2]
    nq = queries * rank
    own_n = nd // nf
    pairs = nd // 2
    bits = nd.bit_length() - 1
    dma = pltpu.SemaphoreType.DMA

    def sems(chunks, lanes):
        return [dma((nd, chunks)), dma((lanes, NA - 1, chunks)), dma((lanes, NA - 1, chunks)),
                dma((NA * max(nb - 1, 1), chunks)), dma((NA * nb, chunks))]

    any_spec = pl.BlockSpec(memory_space=pl.ANY)
    scores, _, _ = pl.pallas_call(
        functools.partial(kernel, nb, nf),
        out_shape=(jax.ShapeDtypeStruct((nf, own_n, nq), F32), jax.ShapeDtypeStruct((nd, tok, kg), BF16),
                   jax.ShapeDtypeStruct((nd, tok, ka), BF16)),
        in_specs=[any_spec] * 7,
        out_specs=(pl.BlockSpec(memory_space=pltpu.VMEM), any_spec, any_spec),
        scratch_shapes=[
            pltpu.VMEM(basis_out.shape, BF16), pltpu.VMEM(basis_in.shape, BF16), pltpu.VMEM((2, 2 * tok, kg), BF16),
            pltpu.VMEM((nd, ni, nj), F32), pltpu.VMEM((2, ni, nj), BF16), pltpu.VMEM((nd, own_n * tok + nq, nj), BF16),
            pltpu.VMEM((pairs, 2 * tok, ni), BF16), pltpu.VMEM((nf - 1, own_n, tok, ni), BF16),
            pltpu.VMEM((pairs, 2 * tok, nj), BF16), pltpu.VMEM((nf - 1, own_n, tok, nj), BF16),
            pltpu.VMEM((own_n, ni, tok), BF16), pltpu.VMEM((nq, ni), F32), pltpu.VMEM((nf - 1, nq, ni), F32),
            pltpu.VMEM((nq, nj), F32), pltpu.VMEM((nf - 1, nq, nj), F32), pltpu.VMEM((ni, nq), F32),
            pltpu.VMEM((ni, nq), F32), pltpu.VMEM((bits + 1, own_n, nq), F32), pltpu.VMEM((bits + nf - 1, own_n, nq), F32),
            *sems(CHUNKS, 1), *sems(1, 1), *sems(1, nb),
            dma((4,)), dma((2,)), dma((2, 2)), dma((pairs, 2)), dma((nf - 1, own_n)), dma((pairs, 2)), dma((nf - 1, own_n)),
            dma((nf - 1,)), dma((nf - 1,)), dma((nf - 1,)), dma((nf - 1,)), dma((bits + nf - 1,)), dma((bits + nf - 1,)),
        ],
        compiler_params=pltpu.CompilerParams(
            collective_id=0, has_side_effects=True, vmem_limit_bytes=63 * 1024 * 1024),
    )(grad_out.reshape(tok, kg), act_in.reshape(tok, ka), basis_out, basis_in, eigen_vals,
      query_out.reshape(nq, kg), query_in.reshape(nq, ka))
    f = lax.axis_index("factor")
    scores = scores.reshape(nf, own_n, queries, rank).sum(-1)
    whole = scores.transpose(1, 0, 2).reshape(nd, queries)
    return lax.dynamic_slice_in_dim(whole, f * own_n, own_n, 0)


def solution(mesh):
    in_specs = (
        P("dp", None, "factor"),
        P("dp", None, "factor"),
        P("factor", "dp"),
        P("factor", "dp"),
        P("dp", None),
        P(None, None, "factor"),
        P(None, None, "factor"),
    )
    body = functools.partial(shards, mesh.shape["dp"], mesh.shape["factor"])
    return jax.shard_map(body, mesh=mesh, in_specs=in_specs, out_specs=P("factor", None), check_vma=False)
```

time: 485 us -> 390 us (0.80)
  Pallas kernels: 0 us -> 388 us
  waiting for transfers between devices: 288 us -> 0 us
  matrix products: 138 us -> 0 us
  blocking collectives: 31.8 us -> 0 us
  between operations: 14.9 us -> 0.04 us
  other arithmetic: 11.7 us -> 0.11 us
    pallas_call x0 -> x1, Pallas kernels: none -> 388 us  [shards(): pl.pallas_call(functools.partial(kernel, nb, nf), out_shape=(jax.ShapeDty...]
    all_gather x4 -> x0, waiting for transfers between devices: 269 us -> none  [the longest x1 130 us: shards(): shard_part = lax.all_gather(grad_out, 'dp', axis=0, tiled=True)]
    dot_general x12 -> x0, matrix products: 138 us -> none  [the longest x8 82.3 us: per_sequence(): lax.dot_general(scaled, value_mat, (((1,), (1,)), ((), ())), preferred_el...]
    psum x1 -> x0, blocking collectives: 31.8 us -> none  [shards(): return lax.psum(partial_scores, 'dp')]
    reduce_scatter x2 -> x0, waiting for transfers between devices: 17 us -> none  [the longest x1 17 us: shards(): lax.psum_scatter(act_part.astype(jnp.bfloat16), 'factor', scatter_dimensi...]
    convert_element_type x2 -> x0, other arithmetic: 11.7 us -> none  [the longest x1 11.7 us: shards(): eigen_float = eigen_vals.astype(jnp.float32)]
  transfers between devices with their start and end apart: 7 -> 0, of which waited for: 4 -> 0; matrix products, arithmetic and copies ran while one was open for 14% -> 0% of each run, Pallas kernels for 0% -> 0%
where the time goes in v1:
time: 390 us
  Pallas kernels  388 us (99%)
    pallas_call x1, Pallas kernels, shards(): pl.pallas_call(functools.partial(kernel, nb, nf), out_shape=(jax.ShapeDty...  388 us

profile of v1, /device:TPU:0, one launch (start us, length us, event | category | flops | bytes accessed | tf_op | source)
XLA Modules:
  0.0 389.8 jit_solution(1213049871693834003)
XLA Ops:
  0.0 388.2 %shard_map.73 = (f32[2,8,128]{2,1,0:T(8,128)}, bf16[16,128,7168]{2,1,0:T(8,128)(2,1)}, bf16[16,128,2048]{2,1,0:T(8,128)(2,1)}) custom-call(bf16[128,7168]{1,0:T(8,128)(2,1)} %bitcast.6, bf16[128,2048]{1,0:T(8,128)(2,1)} %bitcast.8, bf16[7168,896]{1,0:T(8,128)(2,1)} %bo.1, bf16[2048,256]{1,0:T(8,128)(2,1)} %bi.1, bf16[896,4096]{1,0:T(8,128)(2,1)} %ev.1, ...), custom_call_target="tpu_custom_call" | custom-call | tf_op jit(solution)/shard_map/pallas_call | solution.py:469
  388.2 0.8 reshape.22
  389.0 0.1 reduce_sum.9
  389.2 0.6 constant_dynamic-slice_fusion
  (1 shorter events, 0.0 us)
